TPU v7x, 32 devices: a whole 2x2x4 slice. The times are simulated.
32 devices in a mesh: pipe: 16 (over z, y, core), ctx: 2 (over x).
Axes of the slice: x: 2, y: 2, z: 4, core: 2. Of those that a mesh axis runs over, the one named last changes fastest.
Arguments:
- query: bfloat16 [16, 256, 8192], P('pipe', 'ctx'), may hold values from -6 to 6
- inner: bfloat16 [16, 256, 8192], P('pipe', 'ctx'), may hold values from -6 to 6
- out_grad: bfloat16 [16, 256, 8192], P('pipe', 'ctx'), may hold values from -6 to 6
- filters: float32 [16, 7, 8192], P('pipe'), as said below
- trace_lengths: int32 [16, 2], P('pipe'), may hold values from 1 to 192, 256 in all within a row
Outputs:
- passed_grad: bfloat16 [2, 16, 256, 8192], P(None, 'pipe', 'ctx')
- filter_grad: float32 [16, 7, 8192], P('pipe', None, 'ctx')
Inputs may be any that keep to these rules, and one draw needn't show every extreme that they name: filters of section s and section 15 - s are equal (the same layer).
All inputs are finite; a program needn't handle non-finite values.
Results may differ from a plain program's by a relative error of at most 0.0041.
Values may be sent and summed in bfloat16 or wider, within the bound.
A program may use at most 128 MiB of HBM per device.

v0:
```python
import jax
import jax.numpy as jnp
from jax import lax
from jax.sharding import PartitionSpec as P


def passed_along(x, axis, by):
    devices = lax.axis_size(axis)
    pairs = [(i, i + by) for i in range(devices) if 0 <= i + by < devices]
    return lax.ppermute(x, axis, pairs)


def swapped(x, axis, distance):
    return lax.ppermute(x, axis, [(i, i ^ 1 << distance) for i in range(lax.axis_size(axis))])


def seg_of(pos, ends):
    return jnp.sum((pos[:, None] >= ends[None, :]).astype(jnp.int32), axis=1)


def local_grads(inner, out_grad, gz, taps_in, inner_left, gz_right, ends):
    rows = inner.shape[0]
    width = inner.shape[1]
    taps_count = taps_in.shape[0]
    inner_ext = jnp.concatenate([inner_left, inner], axis=0).astype(jnp.float32)
    gz_ext = jnp.concatenate([gz, gz_right], axis=0).astype(jnp.float32)
    pos = jnp.arange(rows, dtype=jnp.int32)
    seg = seg_of(pos, ends)
    out_f = out_grad.astype(jnp.float32)
    gz_f = gz_ext[:rows]
    zsum = jnp.zeros((rows, width), jnp.float32)
    usum = jnp.zeros((rows, width), jnp.float32)
    taps = []
    for j in range(taps_count):
        back_u = inner_ext[taps_count - 1 - j : taps_count - 1 - j + rows]
        mask_b = (seg == seg_of(pos - j, ends)).astype(jnp.float32)[:, None]
        zsum = zsum + taps_in[j][None, :] * back_u * mask_b
        taps.append(jnp.sum(gz_f * back_u * mask_b, axis=0))
        ahead_g = gz_ext[j : j + rows]
        mask_a = (seg == seg_of(pos + j, ends)).astype(jnp.float32)[:, None]
        usum = usum + taps_in[j][None, :] * ahead_g * mask_a
    grad_q = (out_f * zsum).astype(jnp.bfloat16)
    grad_u = usum.astype(jnp.bfloat16)
    return (grad_q, grad_u, jnp.stack(taps))


def local(query, inner, out_grad, filters, trace_lengths):
    taps_count = filters.shape[1]
    ends = jnp.cumsum(trace_lengths[0])
    moved = (
        lax.all_to_all(query, "ctx", split_axis=2, concat_axis=1, tiled=True),
        lax.all_to_all(inner, "ctx", split_axis=2, concat_axis=1, tiled=True),
        lax.all_to_all(out_grad, "ctx", split_axis=2, concat_axis=1, tiled=True),
    )
    q_cols = moved[0][0]
    u_cols = moved[1][0]
    g_cols = moved[2][0]
    width = q_cols.shape[1]
    start = lax.axis_index("ctx") * width
    taps_in = lax.dynamic_slice_in_dim(filters[0], start, width, 1)
    gz = (g_cols.astype(jnp.float32) * q_cols.astype(jnp.float32)).astype(jnp.bfloat16)
    padding = jnp.zeros((taps_count - 1, width), jnp.bfloat16)
    grad_q, grad_u, filter_part = local_grads(u_cols, g_cols, gz, taps_in, padding, padding, ends)
    returned = (
        lax.all_to_all(grad_q[None], "ctx", split_axis=1, concat_axis=2, tiled=True),
        lax.all_to_all(grad_u[None], "ctx", split_axis=1, concat_axis=2, tiled=True),
    )
    grad_q = returned[0][0]
    grad_u = returned[1][0]
    stacked = jnp.stack([grad_q, grad_u])[:, None]
    passed_grad = passed_along(stacked, "pipe", -1)
    partner = filter_part
    for bit in range(lax.axis_size("pipe").bit_length() - 1):
        partner = swapped(partner, "pipe", bit)
    filter_grad = filter_part + partner
    return (passed_grad, filter_grad[None])


def solution(mesh):
    in_specs = (
        P("pipe", "ctx", None),
        P("pipe", "ctx", None),
        P("pipe", "ctx", None),
        P("pipe", None, None),
        P("pipe", None),
    )
    out_specs = (P(None, "pipe", "ctx", None), P("pipe", None, "ctx"))
    return jax.shard_map(local, mesh=mesh, in_specs=in_specs, out_specs=out_specs, check_vma=False)
```

profile of v0, /device:TPU:4, one launch (start us, length us, event | category | flops | bytes accessed | tf_op | source)
XLA Modules:
  0.0 446.3 jit_solution(17359591299817409962)
XLA Ops:
  0.6 9.5 %copy.29 = bf16[1,128,8192]{1,0,2:T(2,128)(2,1)} copy(bf16[1,128,8192]{2,1,0:T(8,128)(2,1)} %param.7) | data formatting | bytes 4194304 | tf_op args[2]
  10.6 45.2 %reduce.1 = bf16[8192,128]{1,0:T(8,128)(2,1)S(1)} reduce(bf16[8192,1,128]{2,1,0:T(2,128)(2,1)} %bitcast.66, bf16[]{:T(256)} %broadcast.118), dimensions={1}, to_apply=%bitcast.52.reduce_sub_computation | reduce | bytes 4194306
  57.4 4.2 all-to-all-start
  61.7 9.5 %copy.36 = bf16[1,128,8192]{1,0,2:T(2,128)(2,1)} copy(bf16[1,128,8192]{2,1,0:T(8,128)(2,1)} %param.5) | data formatting | bytes 4194304 | tf_op args[0]
  71.2 46.5 %reduce = bf16[8192,128]{1,0:T(8,128)(2,1)} reduce(bf16[8192,1,128]{2,1,0:T(2,128)(2,1)} %bitcast.74, bf16[]{:T(256)} %broadcast.118), dimensions={1}, to_apply=%bitcast.50.reduce_sub_computation | reduce | bytes 4194306
  120.5 9.5 %copy.32 = bf16[1,128,8192]{1,0,2:T(2,128)(2,1)} copy(bf16[1,128,8192]{2,1,0:T(8,128)(2,1)} %param.6) | data formatting | bytes 4194304 | tf_op args[1]
  130.0 46.6 %reduce.2 = bf16[8192,128]{1,0:T(8,128)(2,1)} reduce(bf16[8192,1,128]{2,1,0:T(2,128)(2,1)} %bitcast.75, bf16[]{:T(256)} %broadcast.118), dimensions={1}, to_apply=%bitcast.56.reduce_sub_computation | reduce | bytes 4194306
  179.8 4.8 %all-to-all-start.3 = ((bf16[2,2,262144]{2,1,0:T(2,128)(2,1)}), bf16[2,2,262144]{2,1,0:T(2,128)(2,1)}, u32[]{:S(2)}, u32[]{:S(2)}) async-start(bf16[2,2,262144]{2,1,0:T(2,128)(2,1)} %reshape.180), calls=%async_computation.3 | async-start | bytes 4194304 | tf_op jit(solution)/shard_map/all_to_all | solution.py:51
  192.5 5.6 %copy.31 = f32[1,2,128,4096]{3,2,1,0:T(8,128)} copy(f32[1,2,128,4096]{2,3,1,0:T(8,128)} %convert_bitcast_fusion.1) | data formatting | bytes 8388608 | tf_op jit(solution)/shard_map/convert_element_type | solution.py:29
  198.1 11.7 %all-to-all-done.3 = bf16[2,2,262144]{2,1,0:T(2,128)(2,1)} async-done(((bf16[2,2,262144]{2,1,0:T(2,128)(2,1)}), bf16[2,2,262144]{2,1,0:T(2,128)(2,1)}, u32[]{:S(2)}, u32[]{:S(2)}) %all-to-all-start.3) | async-done | bytes 2097184 | tf_op jit(solution)/shard_map/all_to_all | solution.py:51
  209.8 3.9 all-to-all-start.1
  213.8 4.3 reshape.181
  222.8 5.6 %copy.38 = f32[1,2,128,4096]{3,2,1,0:T(8,128)} copy(f32[1,2,128,4096]{2,3,1,0:T(8,128)} %convert_bitcast_fusion) | data formatting | bytes 8388608 | tf_op jit(solution)/shard_map/convert_element_type | solution.py:61
  228.4 9.5 %all-to-all-done.1 = bf16[2,2,262144]{2,1,0:T(2,128)(2,1)S(1)} async-done(((bf16[2,2,262144]{2,1,0:T(2,128)(2,1)}), bf16[2,2,262144]{2,1,0:T(2,128)(2,1)S(1)}, u32[]{:S(2)}, u32[]{:S(2)}) %all-to-all-start.1) | async-done | bytes 2097184 | tf_op jit(solution)/shard_map/all_to_all | solution.py:52
  247.8 4.0 fusion.13
  254.7 5.0 %fusion.14 = bf16[256,4096]{1,0:T(8,128)(2,1)S(1)} fusion(f32[1,2,128,4096]{3,2,1,0:T(8,128)S(1)} %copy-done.1, f32[262,4096]{1,0:T(8,128)S(1)} %get-tuple-element.60, f32[256]{0:T(256)S(1)} %get-tuple-element.42, f32[4096]{0:T(1024)S(1)} %bitcast.97, f32[256]{0:T(256)S(1)} %get-tuple-element.43, f32[4096]{0:T(1024)S(1)} %bitcast.87, ...), kind=kLoop, calls=%fused_computation.25 | loop fusion | flops 22020096 | bytes 35772416 | tf_op jit(solution)/shard_map/convert_element_type | solution.py:42
  259.8 6.8 %copy.48 = bf16[1,256,4096]{2,0,1:T(2,128)(2,1)} copy(bf16[1,256,4096]{2,1,0:T(8,128)(2,1)S(1)} %bitcast.78) | data formatting | bytes 4194304 | tf_op jit(solution)/shard_map/broadcast_in_dim | solution.py:65
  266.6 13.5 %reduce.4 = bf16[256,4096]{1,0:T(8,128)(2,1)S(1)} reduce(bf16[256,1,4096]{2,1,0:T(2,128)(2,1)} %bitcast.71, bf16[]{:T(256)} %broadcast.118), dimensions={1}, to_apply=%bitcast.63.reduce_sub_computation | reduce | bytes 4194306
  286.6 15.7 %fusion.15 = bf16[1,256,4096]{2,1,0:T(8,128)(2,1)S(1)} fusion(f32[256]{0:T(256)S(1)} %get-tuple-element.36, f32[262,4096]{1,0:T(8,128)} %get-tuple-element.59, f32[4096]{0:T(1024)S(1)} %bitcast.98, f32[256]{0:T(256)S(1)} %get-tuple-element.37, f32[4096]{0:T(1024)S(1)} %bitcast.88, f32[256]{0:T(256)S(1)} %get-tuple-element.38, f32[4096]{0:T(1024)S(1)} %bitcast.90, ...), kind=kLoop, calls=%fused_computation.35 | loop fusion | flops 20971520 | bytes 31578112 | tf_op jit(solution)/shard_map/broadcast_in_dim | solution.py:66
  302.3 6.8 %copy.47 = bf16[1,256,4096]{2,0,1:T(2,128)(2,1)} copy(bf16[1,256,4096]{2,1,0:T(8,128)(2,1)S(1)} %fusion.15) | data formatting | bytes 4194304 | tf_op jit(solution)/shard_map/broadcast_in_dim | solution.py:66
  309.2 14.9 %reduce.3 = bf16[256,4096]{1,0:T(8,128)(2,1)} reduce(bf16[256,1,4096]{2,1,0:T(2,128)(2,1)} %bitcast.67, bf16[]{:T(256)} %broadcast.118), dimensions={1}, to_apply=%bitcast.62.reduce_sub_computation | reduce | bytes 4194306
  327.8 4.9 %all-to-all-start.4 = ((bf16[2,2,262144]{2,1,0:T(2,128)(2,1)}), bf16[2,2,262144]{2,1,0:T(2,128)(2,1)}, u32[]{:S(2)}, u32[]{:S(2)}) async-start(bf16[2,2,262144]{2,1,0:T(2,128)(2,1)} %reshape.184), calls=%async_computation.4 | async-start | bytes 4194304 | tf_op jit(solution)/shard_map/all_to_all | solution.py:66
  336.0 4.5 %copy.43 = bf16[1,256,4096]{2,1,0:T(8,128)(2,1)S(1)} copy(bf16[1,256,4096]{2,0,1:T(2,128)(2,1)} %bitcast.72) | data formatting | bytes 4194304
  343.0 13.0 %all-to-all-done.4 = bf16[2,2,262144]{2,1,0:T(2,128)(2,1)} async-done(((bf16[2,2,262144]{2,1,0:T(2,128)(2,1)}), bf16[2,2,262144]{2,1,0:T(2,128)(2,1)}, u32[]{:S(2)}, u32[]{:S(2)}) %all-to-all-start.4) | async-done | bytes 2097184 | tf_op jit(solution)/shard_map/all_to_all | solution.py:66
  356.0 4.3 reshape.185
  360.4 4.5 %copy.44 = bf16[1,256,4096]{2,1,0:T(8,128)(2,1)S(1)} copy(bf16[1,256,4096]{2,0,1:T(2,128)(2,1)} %bitcast.73) | data formatting | bytes 4194304
  367.3 4.8 %maximum_bitcast_fusion = bf16[2,1,128,8192]{2,3,0,1:T(8,128)(2,1)} fusion(bf16[1,128,8192]{1,2,0:T(8,128)(2,1)} %bitcast.84, bf16[1,128,8192]{1,2,0:T(8,128)(2,1)} %bitcast.83), kind=kLoop, calls=%fused_computation.19 | loop fusion | flops 2097152 | bytes 8388608 | tf_op jit(solution)/shard_map/broadcast_in_dim | solution.py:70
  374.1 6.8 %multiply_reduce_fusion = (f32[4096]{0:T(1024)S(1)}, f32[4096]{0:T(1024)S(1)}, f32[4096]{0:T(1024)S(1)}, f32[4096]{0:T(1024)S(1)}, f32[4096]{0:T(1024)S(1)}, /*index=5*/f32[4096]{0:T(1024)S(1)}, f32[4096]{0:T(1024)S(1)}) fusion(f32[262,4096]{1,0:T(8,128)S(1)} %bitcast.65, f32[262,4096]{1,0:T(8,128)} %get-tuple-element.59, f32[256]{0:T(256)S(1)} %get-tuple-element.42, ...), kind=kLoop, calls=%fused_computation.26 | loop fusion | flops 20942848 | bytes 33675264 | tf_op jit(solution)/shard_map/reduce_sum | solution.py:38
  383.5 41.5 %collective-permute-done.2 = f32[7,4096]{1,0:T(8,128)S(1)} collective-permute-done((f32[7,4096]{1,0:T(8,128)S(1)}, f32[7,4096]{1,0:T(8,128)S(1)}, u32[]{:S(2)}, u32[]{:S(2)}) %collective-permute-start.2) | collective-permute-done | bytes 114720 | tf_op jit(solution)/shard_map/ppermute | solution.py:14
  426.6 3.9 collective-permute-done.3
  433.1 5.7 %collective-permute-done.4 = f32[7,4096]{1,0:T(8,128)S(1)} collective-permute-done((f32[7,4096]{1,0:T(8,128)S(1)}, f32[7,4096]{1,0:T(8,128)S(1)}, u32[]{:S(2)}, u32[]{:S(2)}) %collective-permute-start.4) | collective-permute-done | bytes 114720 | tf_op jit(solution)/shard_map/ppermute | solution.py:14
  439.6 6.3 %copy.41 = bf16[2,1,128,8192]{3,2,1,0:T(8,128)(2,1)} copy(bf16[2,1,128,8192]{2,3,0,1:T(8,128)(2,1)} %collective-permute-done) | data formatting | bytes 8388608
  (54 shorter events, 61.5 us)
Async XLA Ops:
  57.4 122.4 %all-to-all-start = ((bf16[2,2,262144]{2,1,0:T(2,128)(2,1)}), bf16[2,2,262144]{2,1,0:T(2,128)(2,1)S(1)}, u32[]{:S(2)}, u32[]{:S(2)}) async-start(bf16[2,2,262144]{2,1,0:T(2,128)(2,1)} %reshape.182), calls=%async_computation | async-start | bytes 4194304 | tf_op jit(solution)/shard_map/all_to_all | solution.py:53
  130.0 49.4 %copy-start.3 = (s32[1,2]{1,0:T(1,128)S(1)}, s32[1,2]{1,0:T(1,128)}, u32[]{:S(2)}) copy-start(s32[1,2]{1,0:T(1,128)} %param.9) | copy-start | bytes 28
  130.0 49.7 %copy-start.2 = (f32[1,7,8192]{2,0,1:T(1,128)S(1)}, f32[1,7,8192]{2,0,1:T(1,128)}, u32[]{:S(2)}) copy-start(f32[1,7,8192]{2,0,1:T(1,128)} %param.8) | copy-start | bytes 688132
  179.8 30.0 %all-to-all-start.3 = ((bf16[2,2,262144]{2,1,0:T(2,128)(2,1)}), bf16[2,2,262144]{2,1,0:T(2,128)(2,1)}, u32[]{:S(2)}, u32[]{:S(2)}) async-start(bf16[2,2,262144]{2,1,0:T(2,128)(2,1)} %reshape.180), calls=%async_computation.3 | async-start | bytes 4194304 | tf_op jit(solution)/shard_map/all_to_all | solution.py:51
  209.8 28.1 %all-to-all-start.1 = ((bf16[2,2,262144]{2,1,0:T(2,128)(2,1)}), bf16[2,2,262144]{2,1,0:T(2,128)(2,1)S(1)}, u32[]{:S(2)}, u32[]{:S(2)}) async-start(bf16[2,2,262144]{2,1,0:T(2,128)(2,1)} %reshape.186), calls=%async_computation.1 | async-start | bytes 4194304 | tf_op jit(solution)/shard_map/all_to_all | solution.py:52
  251.7 2.9 copy-start.1
  254.7 5.1 %copy-start = (f32[262,4096]{1,0:T(8,128)}, f32[262,4096]{1,0:T(8,128)S(1)}, u32[]{:S(2)}) copy-start(f32[262,4096]{1,0:T(8,128)S(1)} %get-tuple-element.60) | copy-start | bytes 12877828
  282.8 44.9 %all-to-all-start.2 = ((bf16[2,2,262144]{2,1,0:T(2,128)(2,1)}), bf16[2,2,262144]{2,1,0:T(2,128)(2,1)S(1)}, u32[]{:S(2)}, u32[]{:S(2)}) async-start(bf16[2,2,262144]{2,1,0:T(2,128)(2,1)} %reshape.188), calls=%async_computation.2 | async-start | bytes 4194304 | tf_op jit(solution)/shard_map/all_to_all | solution.py:65
  327.8 28.3 %all-to-all-start.4 = ((bf16[2,2,262144]{2,1,0:T(2,128)(2,1)}), bf16[2,2,262144]{2,1,0:T(2,128)(2,1)}, u32[]{:S(2)}, u32[]{:S(2)}) async-start(bf16[2,2,262144]{2,1,0:T(2,128)(2,1)} %reshape.184), calls=%async_computation.4 | async-start | bytes 4194304 | tf_op jit(solution)/shard_map/all_to_all | solution.py:66
  367.3 6.7 %slice-start = ((s8[4325376]{0:T(1024)(128)(4,1)}), s8[4194304]{0:T(1024)(128)(4,1)S(1)}, s32[]{:S(2)}) async-start(s8[4325376]{0:T(1024)(128)(4,1)} %bitcast.64), calls=%async_computation.5 | async-start | bytes 8388608
  367.3 6.7 %slice-start.1 = ((s8[4325376]{0:T(1024)(128)(4,1)}), s8[131072]{0:T(1024)(128)(4,1)S(1)}, s32[]{:S(2)}) async-start(s8[4325376]{0:T(1024)(128)(4,1)} %bitcast.64), calls=%async_computation.6 | async-start | bytes 262144
  372.1 67.4 %collective-permute-start = (bf16[2,1,128,8192]{2,3,0,1:T(8,128)(2,1)}, bf16[2,1,128,8192]{2,3,0,1:T(8,128)(2,1)}, u32[]{:S(2)}, u32[]{:S(2)}) collective-permute-start(bf16[2,1,128,8192]{2,3,0,1:T(8,128)(2,1)} %maximum_bitcast_fusion), channel_id=1, source_target_pairs={{2,0},{4,2},{6,4},{8,6},{10,8},{12,10},{14,12},{16,14},{18,16},{20... | collective-permute-start | bytes 12582920 | tf_op jit(solution)/shard_map/ppermute | solution.py:10
  381.1 1.6 collective-permute-start.1
  382.6 42.4 %collective-permute-start.2 = (f32[7,4096]{1,0:T(8,128)S(1)}, f32[7,4096]{1,0:T(8,128)S(1)}, u32[]{:S(2)}, u32[]{:S(2)}) collective-permute-start(f32[7,4096]{1,0:T(8,128)S(1)} %collective-permute-done.1), channel_id=1, source_target_pairs={{0,4},{2,6},{4,0},{6,2},{8,12},{10,14},{12,8},{14,10},{16,20},{18,... | collective-permute-start | bytes 344072 | tf_op jit(solution)/shard_map/ppermute | solution.py:14
  425.0 5.5 %collective-permute-start.3 = (f32[7,4096]{1,0:T(8,128)S(1)}, f32[7,4096]{1,0:T(8,128)S(1)}, u32[]{:S(2)}, u32[]{:S(2)}) collective-permute-start(f32[7,4096]{1,0:T(8,128)S(1)} %collective-permute-done.2), channel_id=1, source_target_pairs={{0,8},{2,10},{4,12},{6,14},{8,0},{10,2},{12,4},{14,6},{16,24},{18,... | collective-permute-start | bytes 344072 | tf_op jit(solution)/shard_map/ppermute | solution.py:14
  430.5 8.3 %collective-permute-start.4 = (f32[7,4096]{1,0:T(8,128)S(1)}, f32[7,4096]{1,0:T(8,128)S(1)}, u32[]{:S(2)}, u32[]{:S(2)}) collective-permute-start(f32[7,4096]{1,0:T(8,128)S(1)} %collective-permute-done.3), channel_id=1, source_target_pairs={{0,16},{2,18},{4,20},{6,22},{8,24},{10,26},{12,28},{14,30},{16,0},... | collective-permute-start | bytes 344072 | tf_op jit(solution)/shard_map/ppermute | solution.py:14
where the time goes:
time: 453 us; the launch traced here: 446 us
  other arithmetic  211 us (47%)
  local copies, waits for them, and re-layouts  119 us (26%)
  waiting for transfers between devices  86.4 us (19%)
  starting transfers between devices  29.2 us (6%)
    unnamed x6, other arithmetic  167 us
    unnamed x30, local copies, waits for them, and re-layouts  80.1 us
    ppermute x4, waiting for transfers between devices, swapped(): lax.ppermute(x, axis, [(i, i ^ 1 << distance) for i in range(lax.axis_siz...  52.1 us
    broadcast_in_dim x1, other arithmetic, local(): grad_u[None]  15.7 us
    all_to_all x1, waiting for transfers between devices, local(): lax.all_to_all(grad_u[None], 'ctx', split_axis=1, concat_axis=2, tiled=True)  13 us
    all_to_all x1, waiting for transfers between devices, local(): lax.all_to_all(query, 'ctx', split_axis=2, concat_axis=1, tiled=True)  11.7 us
    all_to_all x1, waiting for transfers between devices, local(): lax.all_to_all(inner, 'ctx', split_axis=2, concat_axis=1, tiled=True)  9.52 us
  transfers between devices with their start and end apart: 10, of which 7 were waited for; matrix products, arithmetic and copies ran while one was open for 46% of the time, Pallas kernels for 0%

commit v1 on v0

v1 whole, which is shorter than its diff:
```python
import functools

import jax
import jax.numpy as jnp
from jax import lax
from jax.experimental import pallas as pl
from jax.experimental.pallas import tpu as pltpu
from jax.sharding import PartitionSpec as P

MESH = pl.DeviceIdType.MESH
EDGE = 16
LANES = 128
CHUNK = 512


def fold(x):
    return x[: EDGE // 2] + x[EDGE // 2 :]


def rounded_product(a, b):
    return (a.astype(jnp.float32) * b.astype(jnp.float32)).astype(jnp.bfloat16).astype(jnp.float32)


def kernel(
    n_pipe, n_ctx, n_seg,
    lengths, query, inner, out_grad, filters, arrived, summed,
    q_v, u_v, g_v, f_v, u_left, q_right, g_right, u_f, gz_f, masks, parts, staged, dh, dh_in, total, mirrored,
    load_sem, filter_sem, halo_send, halo_recv, out_send, out_recv, edge_send, edge_recv, dh_send, dh_recv, mirror_send, mirror_recv,
):
    taps, _, width = filters.shape
    rows = query.shape[0]
    own = width // n_ctx
    chunks = width // CHUNK
    s = lax.axis_index("pipe")
    c = lax.axis_index("ctx")
    first, last = s == 0, s == n_pipe - 1
    before, after = lax.rem(s + n_pipe - 1, n_pipe), lax.rem(s + 1, n_pipe)
    mirror = n_pipe - 1 - s

    def cols_of(i):
        return pl.ds(pl.multiple_of(i * CHUNK, CHUNK), CHUNK)

    def loads(i):
        cols = cols_of(i)
        return [
            pltpu.make_async_copy(src.at[:, cols], dst.at[:, cols], load_sem.at[k, i])
            for k, (src, dst) in enumerate(((query, q_v), (inner, u_v), (out_grad, g_v)))
        ]

    filter_load = pltpu.make_async_copy(filters, f_v, filter_sem)
    filter_load.start()
    for i in range(2):
        for load in loads(i):
            load.start()

    barrier = pltpu.get_barrier_semaphore()
    for other in (before, after, mirror):
        pl.semaphore_signal(barrier, inc=1, device_id={"pipe": other}, device_id_type=MESH)
    for d in range(1, n_ctx):
        pl.semaphore_signal(barrier, inc=1, device_id={"ctx": lax.rem(c + d, n_ctx)}, device_id_type=MESH)

    ends = []
    for k in range(n_seg):
        ends.append(lengths[0, k] + (ends[-1] if ends else 0))
    pos = c * rows + lax.broadcasted_iota(jnp.int32, (rows + EDGE, LANES), 0)

    def seg_of(at):
        return sum((at >= end).astype(jnp.int32) for end in ends)

    seg = seg_of(pos)
    for j in range(1, taps):
        masks[j - 1] = (seg == seg_of(pos - j)).astype(jnp.float32)

    def back(j, base, mask_at):
        x = u_f[base - j : base - j + EDGE]
        return x if j == 0 else x * masks[j - 1, mask_at : mask_at + EDGE]

    def ahead(j, base, mask_at):
        x = gz_f[base + j : base + j + EDGE]
        return x if j == 0 else x * masks[j - 1, mask_at + j : mask_at + j + EDGE]

    def taps_at(cols):
        return [jnp.broadcast_to(f_v[j, :, cols], (EDGE, LANES)) for j in range(taps)]

    def interior(i):
        def group(l, carry):
            cols = pl.ds(pl.multiple_of(i * CHUNK + l * LANES, LANES), LANES)
            u_f[EDGE : EDGE + rows] = u_v[:, cols].astype(jnp.float32)
            gz_f[:rows] = rounded_product(g_v[:, cols], q_v[:, cols])
            f = taps_at(cols)
            sums = [jnp.zeros((EDGE // 2, LANES), jnp.float32)] * taps
            for at in range(0, rows, EDGE):
                if at > 0:
                    gz = gz_f[at : at + EDGE]
                    z = None
                    for j in range(taps):
                        u = back(j, EDGE + at, at)
                        z = f[j] * u if z is None else z + f[j] * u
                        sums[j] = sums[j] + fold(gz * u)
                    staged[0, at : at + EDGE, cols] = (g_v[at : at + EDGE, cols].astype(jnp.float32) * z).astype(jnp.bfloat16)
                if at < rows - EDGE:
                    z = f[0] * ahead(0, at, at)
                    for j in range(1, taps):
                        z = z + f[j] * ahead(j, at, at)
                    staged[1, at : at + EDGE, cols] = z.astype(jnp.bfloat16)
            for j in range(taps):
                parts[j, :, cols] = sums[j]
            return carry

        lax.fori_loop(0, CHUNK // LANES, group, 0)

    def edges(l, carry):
        cols = pl.ds(pl.multiple_of(l * LANES, LANES), LANES)
        f = taps_at(cols)
        u_f[:EDGE] = u_left[:, cols].astype(jnp.float32)
        u_f[EDGE : 2 * EDGE] = u_v[:EDGE, cols].astype(jnp.float32)
        gz_f[:EDGE] = rounded_product(g_v[rows - EDGE :, cols], q_v[rows - EDGE :, cols])
        gz_f[EDGE : 2 * EDGE] = rounded_product(g_right[:, cols], q_right[:, cols])
        gz = rounded_product(g_v[:EDGE, cols], q_v[:EDGE, cols])
        z = None
        for j in range(taps):
            u = back(j, EDGE, 0)
            z = f[j] * u if z is None else z + f[j] * u
            dh[j : j + 1, cols] = jnp.sum(parts[j, :, cols] + fold(gz * u), axis=0, keepdims=True)
        staged[0, :EDGE, cols] = (g_v[:EDGE, cols].astype(jnp.float32) * z).astype(jnp.bfloat16)
        z = f[0] * ahead(0, 0, rows - EDGE)
        for j in range(1, taps):
            z = z + f[j] * ahead(j, 0, rows - EDGE)
        staged[1, rows - EDGE :, cols] = z.astype(jnp.bfloat16)
        return carry

    def sends(i):
        cols = cols_of(i)
        return [
            pltpu.make_async_remote_copy(
                src_ref=staged.at[k, at, cols], dst_ref=arrived.at[k, 0, at, cols],
                send_sem=out_send.at[k, i], recv_sem=out_recv.at[k, i],
                device_id={"pipe": before}, device_id_type=MESH,
            )
            for k, at in enumerate((pl.ds(EDGE, rows - EDGE), pl.ds(0, rows - EDGE)))
        ]

    def edge_sends():
        return [
            pltpu.make_async_remote_copy(
                src_ref=staged.at[k, at], dst_ref=arrived.at[k, 0, at],
                send_sem=edge_send.at[k], recv_sem=edge_recv.at[k],
                device_id={"pipe": before}, device_id_type=MESH,
            )
            for k, at in enumerate((pl.ds(0, EDGE), pl.ds(rows - EDGE, EDGE)))
        ]

    def halo(k, src, dst, other):
        return pltpu.make_async_remote_copy(
            src_ref=src, dst_ref=dst, send_sem=halo_send.at[k], recv_sem=halo_recv.at[k],
            device_id={"ctx": other}, device_id_type=MESH,
        )

    to_right = [halo(0, inner.at[pl.ds(rows - EDGE, EDGE)], u_left, lax.rem(c + 1, n_ctx))]
    to_left = [
        halo(1, query.at[pl.ds(0, EDGE)], q_right, lax.rem(c + n_ctx - 1, n_ctx)),
        halo(2, out_grad.at[pl.ds(0, EDGE)], g_right, lax.rem(c + n_ctx - 1, n_ctx)),
    ]

    def step(i, carry):
        @pl.when(i + 2 < chunks)
        def _():
            for load in loads(i + 2):
                load.start()

        for load in loads(i):
            load.wait()
        interior(i)

        @pl.when(jnp.logical_not(first))
        def _():
            for send in sends(i):
                send.start()

        return carry

    filter_load.wait()
    for load in loads(2):
        load.start()
    for load in loads(0):
        load.wait()
    interior(0)
    pl.semaphore_wait(barrier, 3 + n_ctx - 1)

    @pl.when(jnp.logical_not(first))
    def _():
        for send in sends(0):
            send.start()

    @pl.when(c < n_ctx - 1)
    def _():
        for send in to_right:
            send.start()

    @pl.when(c > 0)
    def _():
        for send in to_left:
            send.start()

    @pl.when(c == 0)
    def _():
        u_left[...] = jnp.zeros_like(u_left)

    @pl.when(c == n_ctx - 1)
    def _():
        q_right[...] = jnp.zeros_like(q_right)
        g_right[...] = jnp.zeros_like(g_right)

    lax.fori_loop(1, chunks, step, 0)

    @pl.when(c > 0)
    def _():
        for send in to_right:
            send.wait_recv()

    @pl.when(c < n_ctx - 1)
    def _():
        for send in to_left:
            send.wait_recv()

    dh[...] = jnp.zeros_like(dh)
    lax.fori_loop(0, width // LANES, edges, 0)

    @pl.when(jnp.logical_not(first))
    def _():
        for send in edge_sends():
            send.start()

    shares = []
    for d in range(1, n_ctx):
        other = lax.rem(c + d, n_ctx)
        shares.append(
            pltpu.make_async_remote_copy(
                src_ref=dh.at[:, pl.ds(pl.multiple_of(other * own, own), own)], dst_ref=dh_in.at[d - 1],
                send_sem=dh_send.at[d - 1], recv_sem=dh_recv.at[d - 1],
                device_id={"ctx": other}, device_id_type=MESH,
            )
        )
    for share in shares:
        share.start()
    for share in shares:
        share.wait_recv()
    mine = dh[:, pl.ds(pl.multiple_of(c * own, own), own)]
    for d in range(1, n_ctx):
        mine = mine + dh_in[d - 1]
    total[...] = mine
    swap = pltpu.make_async_remote_copy(
        src_ref=total, dst_ref=mirrored, send_sem=mirror_send, recv_sem=mirror_recv,
        device_id={"pipe": mirror}, device_id_type=MESH,
    )
    swap.start()

    @pl.when(last)
    def _():
        arrived[...] = jnp.zeros_like(arrived)

    swap.wait_recv()
    summed[...] = total[...] + mirrored[...]
    swap.wait_send()
    for share in shares:
        share.wait_send()

    @pl.when(c < n_ctx - 1)
    def _():
        for send in to_right:
            send.wait_send()

    @pl.when(c > 0)
    def _():
        for send in to_left:
            send.wait_send()

    @pl.when(jnp.logical_not(first))
    def _():
        def drained(i, carry):
            for send in sends(i):
                send.wait_send()
            return carry

        lax.fori_loop(0, chunks, drained, 0)
        for send in edge_sends():
            send.wait_send()

    @pl.when(jnp.logical_not(last))
    def _():
        def landed(i, carry):
            for send in sends(i):
                send.wait_recv()
            return carry

        lax.fori_loop(0, chunks, landed, 0)
        for send in edge_sends():
            send.wait_recv()


def finish(arrived, summed, passed, grad, sem):
    copies = [pltpu.make_async_copy(arrived.at[k], passed.at[k], sem.at[k]) for k in range(2)]
    for copy in copies:
        copy.start()
    for j in range(grad.shape[0]):
        grad[j] = summed[j : j + 1]
    for copy in copies:
        copy.wait()


def local(n_pipe, n_ctx, query, inner, out_grad, filters, trace_lengths):
    _, rows, width = query.shape
    taps = filters.shape[1]
    own = width // n_ctx
    chunks = width // CHUNK
    anywhere = pl.BlockSpec(memory_space=pl.ANY)
    vmem = pl.BlockSpec(memory_space=pltpu.VMEM)
    f32, bf16, dma = jnp.float32, jnp.bfloat16, pltpu.SemaphoreType.DMA
    arrived, summed = pl.pallas_call(
        functools.partial(kernel, n_pipe, n_ctx, trace_lengths.shape[1]),
        out_shape=(pltpu.VMEM((2, 1, rows, width), bf16), pltpu.VMEM((8, own), f32)),
        in_specs=[pl.BlockSpec(memory_space=pltpu.SMEM)] + [anywhere] * 4,
        out_specs=(vmem, vmem),
        scratch_shapes=[
            pltpu.VMEM((rows, width), bf16),
            pltpu.VMEM((rows, width), bf16),
            pltpu.VMEM((rows, width), bf16),
            pltpu.VMEM((taps, 1, width), f32),
            pltpu.VMEM((EDGE, width), bf16),
            pltpu.VMEM((EDGE, width), bf16),
            pltpu.VMEM((EDGE, width), bf16),
            pltpu.VMEM((rows + EDGE, LANES), f32),
            pltpu.VMEM((rows + EDGE, LANES), f32),
            pltpu.VMEM((taps - 1, rows + EDGE, LANES), f32),
            pltpu.VMEM((taps, EDGE // 2, width), f32),
            pltpu.VMEM((2, rows, width), bf16),
            pltpu.VMEM((8, width), f32),
            pltpu.VMEM((n_ctx - 1, 8, own), f32),
            pltpu.VMEM((8, own), f32),
            pltpu.VMEM((8, own), f32),
            dma((3, chunks)),
            dma,
            dma((3,)),
            dma((3,)),
            dma((2, chunks)),
            dma((2, chunks)),
            dma((2,)),
            dma((2,)),
            dma((n_ctx - 1,)),
            dma((n_ctx - 1,)),
            dma,
            dma,
        ],
        compiler_params=pltpu.CompilerParams(collective_id=0, has_side_effects=True, vmem_limit_bytes=48 * 1024 * 1024),
        name="grads_passed_on",
    )(trace_lengths, query[0], inner[0], out_grad[0], jnp.swapaxes(filters, 0, 1))
    passed, grad = pl.pallas_call(
        finish,
        out_shape=(
            jax.ShapeDtypeStruct((2, 1, rows, width), bf16),
            jax.ShapeDtypeStruct((taps, 1, own), f32),
        ),
        in_specs=[anywhere, vmem],
        out_specs=(anywhere, vmem),
        scratch_shapes=[dma((2,))],
        name="results_written",
    )(arrived, summed)
    return passed, jnp.swapaxes(grad, 0, 1)


def solution(mesh):
    in_specs = (
        P("pipe", "ctx", None),
        P("pipe", "ctx", None),
        P("pipe", "ctx", None),
        P("pipe", None, None),
        P("pipe", None),
    )
    out_specs = (P(None, "pipe", "ctx", None), P("pipe", None, "ctx"))
    run = functools.partial(local, mesh.shape["pipe"], mesh.shape["ctx"])
    return jax.shard_map(run, mesh=mesh, in_specs=in_specs, out_specs=out_specs, check_vma=False)
```

time: 453 us -> 193 us (0.43)
  the two profiles are of different devices: /device:TPU:4 before, /device:TPU:1 now
where the time goes in v1:
time: 193 us; the launch traced here: 191 us
  Pallas kernels  186 us (96%)
  local copies, waits for them, and re-layouts  4.15 us (2%)
    pallas_call x1, Pallas kernels, local(): pl.pallas_call(finish, out_shape=(jax.ShapeDtypeStruct((2, 1, rows, width...  130 us
    pallas_call x1, Pallas kernels, local(): pl.pallas_call(functools.partial(kernel, n_pipe, n_ctx, trace_lengths.sha...  56.6 us
    unnamed x8, local copies, waits for them, and re-layouts  4.15 us

profile of v1, /device:TPU:1, one launch (start us, length us, event | category | flops | bytes accessed | tf_op | source)
XLA Modules:
  0.0 191.1 jit_solution(737655580620405758)
XLA Ops:
  0.6 0.0 copy-start.1
  0.6 0.9 copy-done.1
  1.6 0.0 copy-start.3
  1.6 0.7 copy-done.3
  2.2 56.6 %grads_passed_on.1 = (bf16[2,1,128,8192]{3,2,1,0:T(8,128)(2,1)S(1)}, f32[8,4096]{1,0:T(8,128)S(1)}) custom-call(s32[1,2]{1,0:T(1,128)S(1)} %copy-done.3, bf16[128,8192]{1,0:T(8,128)(2,1)} %bitcast.6, bf16[128,8192]{1,0:T(8,128)(2,1)} %bitcast.7, bf16[128,8192]{1,0:T(8,128)(2,1)} %bitcast.8, f32[7,1,8192]{2,1,0:T(1,128)S(1)} %bitcast.5), custom_call_target="tpu_custom_call" | custom-call | tf_op jit(solution)/shard_map/grads_passed_on/pallas_call | solution.py:319
  58.8 0.0 copy-start
  58.9 1.9 %copy-done = bf16[2,1,128,8192]{3,2,1,0:T(8,128)(2,1)} copy-done((bf16[2,1,128,8192]{3,2,1,0:T(8,128)(2,1)}, bf16[2,1,128,8192]{3,2,1,0:T(8,128)(2,1)S(1)}, u32[]{:S(2)}) %copy-start) | copy-done | bytes 4194328
  60.8 0.0 copy-start.2
  60.8 0.6 copy-done.2
  61.4 129.7 %results_written.1 = (bf16[2,1,128,8192]{3,2,1,0:T(8,128)(2,1)}, f32[7,1,4096]{2,1,0:T(1,128)}) custom-call(bf16[2,1,128,8192]{3,2,1,0:T(8,128)(2,1)} %copy-done, f32[8,4096]{1,0:T(8,128)} %copy-done.2), custom_call_target="tpu_custom_call" | custom-call | tf_op jit(solution)/shard_map/results_written/pallas_call | solution.py:357
Async XLA Ops:
  0.6 0.9 copy-start.1
  1.6 0.7 copy-start.3
  58.8 1.9 %copy-start = (bf16[2,1,128,8192]{3,2,1,0:T(8,128)(2,1)}, bf16[2,1,128,8192]{3,2,1,0:T(8,128)(2,1)S(1)}, u32[]{:S(2)}) copy-start(bf16[2,1,128,8192]{3,2,1,0:T(8,128)(2,1)S(1)} %get-tuple-element.6.arrived) | copy-start | bytes 12582916
  60.8 0.6 copy-start.2

commit v2 on v1

--- a/solution.py
+++ b/solution.py
@@ -260,7 +260,9 @@
         arrived[...] = jnp.zeros_like(arrived)
 
     swap.wait_recv()
-    summed[...] = total[...] + mirrored[...]
+    both = total[...] + mirrored[...]
+    for j in range(taps):
+        summed[j] = both[j : j + 1]
     swap.wait_send()
     for share in shares:
         share.wait_send()
@@ -296,16 +298,6 @@
         lax.fori_loop(0, chunks, landed, 0)
         for send in edge_sends():
             send.wait_recv()
-
-
-def finish(arrived, summed, passed, grad, sem):
-    copies = [pltpu.make_async_copy(arrived.at[k], passed.at[k], sem.at[k]) for k in range(2)]
-    for copy in copies:
-        copy.start()
-    for j in range(grad.shape[0]):
-        grad[j] = summed[j : j + 1]
-    for copy in copies:
-        copy.wait()
 
 
 def local(n_pipe, n_ctx, query, inner, out_grad, filters, trace_lengths):
@@ -318,7 +310,7 @@
     f32, bf16, dma = jnp.float32, jnp.bfloat16, pltpu.SemaphoreType.DMA
     arrived, summed = pl.pallas_call(
         functools.partial(kernel, n_pipe, n_ctx, trace_lengths.shape[1]),
-        out_shape=(pltpu.VMEM((2, 1, rows, width), bf16), pltpu.VMEM((8, own), f32)),
+        out_shape=(pltpu.VMEM((2, 1, rows, width), bf16), pltpu.VMEM((taps, 1, own), f32)),
         in_specs=[pl.BlockSpec(memory_space=pltpu.SMEM)] + [anywhere] * 4,
         out_specs=(vmem, vmem),
         scratch_shapes=[
@@ -354,18 +346,7 @@
         compiler_params=pltpu.CompilerParams(collective_id=0, has_side_effects=True, vmem_limit_bytes=48 * 1024 * 1024),
         name="grads_passed_on",
     )(trace_lengths, query[0], inner[0], out_grad[0], jnp.swapaxes(filters, 0, 1))
-    passed, grad = pl.pallas_call(
-        finish,
-        out_shape=(
-            jax.ShapeDtypeStruct((2, 1, rows, width), bf16),
-            jax.ShapeDtypeStruct((taps, 1, own), f32),
-        ),
-        in_specs=[anywhere, vmem],
-        out_specs=(anywhere, vmem),
-        scratch_shapes=[dma((2,))],
-        name="results_written",
-    )(arrived, summed)
-    return passed, jnp.swapaxes(grad, 0, 1)
+    return arrived, jnp.swapaxes(summed, 0, 1)
 
 
 def solution(mesh):

time: 193 us -> 63.7 us (0.33)
  the two profiles are of different devices: /device:TPU:1 before, /device:TPU:7 now
where the time goes in v2:
time: 63.7 us; the launch traced here: 63.5 us
  Pallas kernels  58.6 us (92%)
  local copies, waits for them, and re-layouts  4.25 us (7%)
  between operations  0.65 us (1%)
    pallas_call x1, Pallas kernels, local(): pl.pallas_call(functools.partial(kernel, n_pipe, n_ctx, trace_lengths.sha...  58.6 us
    unnamed x6, local copies, waits for them, and re-layouts  4.25 us

profile of v2, /device:TPU:7, one launch (start us, length us, event | category | flops | bytes accessed | tf_op | source)
XLA Modules:
  0.0 63.5 jit_solution(1385366723923910657)
XLA Ops:
  0.6 0.0 copy-start
  0.6 0.9 %copy-done = f32[1,7,8192]{2,0,1:T(1,128)S(1)} copy-done((f32[1,7,8192]{2,0,1:T(1,128)S(1)}, f32[1,7,8192]{2,0,1:T(1,128)}, u32[]{:S(2)}) %copy-start) | copy-done | bytes 229400
  1.6 0.0 copy-start.1
  1.6 0.7 %copy-done.1 = s32[1,2]{1,0:T(1,128)S(1)} copy-done((s32[1,2]{1,0:T(1,128)S(1)}, s32[1,2]{1,0:T(1,128)}, u32[]{:S(2)}) %copy-start.1) | copy-done | bytes 32
  2.2 58.6 %grads_passed_on.1 = (bf16[2,1,128,8192]{3,2,1,0:T(8,128)(2,1)S(1)}, f32[7,1,4096]{2,1,0:T(1,128)S(1)}) custom-call(s32[1,2]{1,0:T(1,128)S(1)} %copy-done.1, bf16[128,8192]{1,0:T(8,128)(2,1)} %bitcast.7, bf16[128,8192]{1,0:T(8,128)(2,1)} %bitcast.8, bf16[128,8192]{1,0:T(8,128)(2,1)} %bitcast.9, f32[7,1,8192]{2,1,0:T(1,128)S(1)} %bitcast.6), custom_call_target="tpu_custom_call" | custom-call | tf_op jit(solution)/shard_map/grads_passed_on/pallas_call | solution.py:311
  60.8 2.0 %copy.9 = bf16[2,1,128,8192]{3,2,1,0:T(8,128)(2,1)} copy(bf16[2,1,128,8192]{3,2,1,0:T(8,128)(2,1)S(1)} %get-tuple-element.6) | data formatting | bytes 8388608
  62.8 0.6 %copy.10 = f32[1,7,4096]{2,0,1:T(1,128)} copy(f32[1,7,4096]{2,0,1:T(1,128)S(1)} %bitcast.5) | data formatting | bytes 229376
Async XLA Ops:
  0.6 0.9 %copy-start = (f32[1,7,8192]{2,0,1:T(1,128)S(1)}, f32[1,7,8192]{2,0,1:T(1,128)}, u32[]{:S(2)}) copy-start(f32[1,7,8192]{2,0,1:T(1,128)} %param.8) | copy-start | bytes 688132
  1.6 0.7 %copy-start.1 = (s32[1,2]{1,0:T(1,128)S(1)}, s32[1,2]{1,0:T(1,128)}, u32[]{:S(2)}) copy-start(s32[1,2]{1,0:T(1,128)} %lengths.1) | copy-start | bytes 28

commit v3 on v2

--- a/solution.py
+++ b/solution.py
@@ -23,14 +23,15 @@
 
 def kernel(
     n_pipe, n_ctx, n_seg,
-    lengths, query, inner, out_grad, filters, arrived, summed,
-    q_v, u_v, g_v, f_v, u_left, q_right, g_right, u_f, gz_f, masks, parts, staged, dh, dh_in, total, mirrored,
-    load_sem, filter_sem, halo_send, halo_recv, out_send, out_recv, edge_send, edge_recv, dh_send, dh_recv, mirror_send, mirror_recv,
+    trace_lengths, query, inner, out_grad, filters, arrived, summed,
+    lengths, q_v, u_v, g_v, f_v, u_left, q_right, g_right, u_f, gz_f, masks, parts, staged, dh, dh_in, total, mirrored,
+    length_sem, load_sem, filter_sem, halo_send, halo_recv, out_send, out_recv, edge_send, edge_recv, dh_send, dh_recv, mirror_send, mirror_recv,
 ):
     taps, _, width = filters.shape
     rows = query.shape[0]
     own = width // n_ctx
     chunks = width // CHUNK
+    early = chunks * 10 // 16
     s = lax.axis_index("pipe")
     c = lax.axis_index("ctx")
     first, last = s == 0, s == n_pipe - 1
@@ -47,6 +48,8 @@
             for k, (src, dst) in enumerate(((query, q_v), (inner, u_v), (out_grad, g_v)))
         ]
 
+    length_load = pltpu.make_async_copy(trace_lengths, lengths, length_sem)
+    length_load.start()
     filter_load = pltpu.make_async_copy(filters, f_v, filter_sem)
     filter_load.start()
     for i in range(2):
@@ -59,6 +62,7 @@
     for d in range(1, n_ctx):
         pl.semaphore_signal(barrier, inc=1, device_id={"ctx": lax.rem(c + d, n_ctx)}, device_id_type=MESH)
 
+    length_load.wait()
     ends = []
     for k in range(n_seg):
         ends.append(lengths[0, k] + (ends[-1] if ends else 0))
@@ -172,7 +176,7 @@
             load.wait()
         interior(i)
 
-        @pl.when(jnp.logical_not(first))
+        @pl.when(jnp.logical_and(jnp.logical_not(first), i < early))
         def _():
             for send in sends(i):
                 send.start()
@@ -225,11 +229,6 @@
 
     dh[...] = jnp.zeros_like(dh)
     lax.fori_loop(0, width // LANES, edges, 0)
-
-    @pl.when(jnp.logical_not(first))
-    def _():
-        for send in edge_sends():
-            send.start()
 
     shares = []
     for d in range(1, n_ctx):
@@ -248,21 +247,34 @@
     mine = dh[:, pl.ds(pl.multiple_of(c * own, own), own)]
     for d in range(1, n_ctx):
         mine = mine + dh_in[d - 1]
-    total[...] = mine
+    half = own // 2
+    total[...] = jnp.concatenate([mine[:, :half], mine[:, half:]], axis=0).astype(jnp.bfloat16)
     swap = pltpu.make_async_remote_copy(
         src_ref=total, dst_ref=mirrored, send_sem=mirror_send, recv_sem=mirror_recv,
         device_id={"pipe": mirror}, device_id_type=MESH,
     )
     swap.start()
 
+    @pl.when(jnp.logical_not(first))
+    def _():
+        def late(i, carry):
+            for send in sends(i):
+                send.start()
+            return carry
+
+        lax.fori_loop(early, chunks, late, 0)
+        for send in edge_sends():
+            send.start()
+
     @pl.when(last)
     def _():
         arrived[...] = jnp.zeros_like(arrived)
 
     swap.wait_recv()
-    both = total[...] + mirrored[...]
+    theirs = mirrored[...].astype(jnp.float32)
     for j in range(taps):
-        summed[j] = both[j : j + 1]
+        summed[j, :, :half] = mine[j : j + 1, :half] + theirs[j : j + 1]
+        summed[j, :, half:] = mine[j : j + 1, half:] + theirs[8 + j : 9 + j]
     swap.wait_send()
     for share in shares:
         share.wait_send()
@@ -305,15 +317,16 @@
     taps = filters.shape[1]
     own = width // n_ctx
     chunks = width // CHUNK
-    anywhere = pl.BlockSpec(memory_space=pl.ANY)
     vmem = pl.BlockSpec(memory_space=pltpu.VMEM)
+    operands = (trace_lengths, query[0], inner[0], out_grad[0], jnp.swapaxes(filters, 0, 1))
     f32, bf16, dma = jnp.float32, jnp.bfloat16, pltpu.SemaphoreType.DMA
     arrived, summed = pl.pallas_call(
         functools.partial(kernel, n_pipe, n_ctx, trace_lengths.shape[1]),
         out_shape=(pltpu.VMEM((2, 1, rows, width), bf16), pltpu.VMEM((taps, 1, own), f32)),
-        in_specs=[pl.BlockSpec(memory_space=pltpu.SMEM)] + [anywhere] * 4,
+        in_specs=[pl.BlockSpec(memory_space=pltpu.HBM)] * 5,
         out_specs=(vmem, vmem),
         scratch_shapes=[
+            pltpu.SMEM(trace_lengths.shape, jnp.int32),
             pltpu.VMEM((rows, width), bf16),
             pltpu.VMEM((rows, width), bf16),
             pltpu.VMEM((rows, width), bf16),
@@ -328,8 +341,9 @@
             pltpu.VMEM((2, rows, width), bf16),
             pltpu.VMEM((8, width), f32),
             pltpu.VMEM((n_ctx - 1, 8, own), f32),
-            pltpu.VMEM((8, own), f32),
-            pltpu.VMEM((8, own), f32),
+            pltpu.VMEM((16, own // 2), bf16),
+            pltpu.VMEM((16, own // 2), bf16),
+            dma,
             dma((3, chunks)),
             dma,
             dma((3,)),
@@ -345,7 +359,7 @@
         ],
         compiler_params=pltpu.CompilerParams(collective_id=0, has_side_effects=True, vmem_limit_bytes=48 * 1024 * 1024),
         name="grads_passed_on",
-    )(trace_lengths, query[0], inner[0], out_grad[0], jnp.swapaxes(filters, 0, 1))
+    )(*(pltpu.with_memory_space_constraint(x, pltpu.HBM) for x in operands))
     return arrived, jnp.swapaxes(summed, 0, 1)
 
 

time: 63.7 us -> 57.9 us (0.909)
  the two profiles are of different devices: /device:TPU:7 before, /device:TPU:1 now
where the time goes in v3:
time: 57.9 us; the launch traced here: 57.7 us
  Pallas kernels  54.4 us (94%)
  local copies, waits for them, and re-layouts  2.66 us (5%)
  between operations  0.64 us (1%)
    pallas_call x1, Pallas kernels, local(): pl.pallas_call(functools.partial(kernel, n_pipe, n_ctx, trace_lengths.sha...  54.4 us
    unnamed x2, local copies, waits for them, and re-layouts  2.66 us

profile of v3, /device:TPU:1, one launch (start us, length us, event | category | flops | bytes accessed | tf_op | source)
XLA Modules:
  0.0 57.7 jit_solution(10540022589820661825)
XLA Ops:
  0.6 54.4 %grads_passed_on.1 = (bf16[2,1,128,8192]{3,2,1,0:T(8,128)(2,1)S(1)}, f32[7,1,4096]{2,1,0:T(1,128)S(1)}) custom-call(s32[1,2]{1,0:T(1,128)} %trace_lengths.1, bf16[128,8192]{1,0:T(8,128)(2,1)} %bitcast.6, bf16[128,8192]{1,0:T(8,128)(2,1)} %bitcast.7, bf16[128,8192]{1,0:T(8,128)(2,1)} %bitcast.8, f32[7,1,8192]{2,1,0:T(1,128)} %bitcast.9), custom_call_target="tpu_custom_call" | custom-call | tf_op jit(solution)/shard_map/grads_passed_on/pallas_call | solution.py:323
  55.0 2.0 %copy.9 = bf16[2,1,128,8192]{3,2,1,0:T(8,128)(2,1)} copy(bf16[2,1,128,8192]{3,2,1,0:T(8,128)(2,1)S(1)} %get-tuple-element.6) | data formatting | bytes 8388608
  57.1 0.6 %copy.10 = f32[1,7,4096]{2,0,1:T(1,128)} copy(f32[1,7,4096]{2,0,1:T(1,128)S(1)} %bitcast.5) | data formatting | bytes 229376

commit v4 on v3

--- a/solution.py
+++ b/solution.py
@@ -10,7 +10,15 @@
 MESH = pl.DeviceIdType.MESH
 EDGE = 16
 LANES = 128
-CHUNK = 512
+FIRST_GROUPS = (256, 256, 512, 1024)
+GROUP = 2048
+
+
+def groups_of(width):
+    sizes = list(FIRST_GROUPS)
+    while sum(sizes) < width:
+        sizes.append(min(GROUP, width - sum(sizes)))
+    return [(sum(sizes[:i]), size) for i, size in enumerate(sizes)]
 
 
 def fold(x):
@@ -30,8 +38,8 @@
     taps, _, width = filters.shape
     rows = query.shape[0]
     own = width // n_ctx
-    chunks = width // CHUNK
-    early = chunks * 10 // 16
+    groups = groups_of(width)
+    early = sum(start < width // 2 for start, _ in groups)
     s = lax.axis_index("pipe")
     c = lax.axis_index("ctx")
     first, last = s == 0, s == n_pipe - 1
@@ -39,7 +47,7 @@
     mirror = n_pipe - 1 - s
 
     def cols_of(i):
-        return pl.ds(pl.multiple_of(i * CHUNK, CHUNK), CHUNK)
+        return pl.ds(*groups[i])
 
     def loads(i):
         cols = cols_of(i)
@@ -52,7 +60,7 @@
     length_load.start()
     filter_load = pltpu.make_async_copy(filters, f_v, filter_sem)
     filter_load.start()
-    for i in range(2):
+    for i in range(3):
         for load in loads(i):
             load.start()
 
@@ -88,7 +96,7 @@
 
     def interior(i):
         def group(l, carry):
-            cols = pl.ds(pl.multiple_of(i * CHUNK + l * LANES, LANES), LANES)
+            cols = pl.ds(pl.multiple_of(groups[i][0] + l * LANES, LANES), LANES)
             u_f[EDGE : EDGE + rows] = u_v[:, cols].astype(jnp.float32)
             gz_f[:rows] = rounded_product(g_v[:, cols], q_v[:, cols])
             f = taps_at(cols)
@@ -111,7 +119,7 @@
                 parts[j, :, cols] = sums[j]
             return carry
 
-        lax.fori_loop(0, CHUNK // LANES, group, 0)
+        lax.fori_loop(0, groups[i][1] // LANES, group, 0)
 
     def edges(l, carry):
         cols = pl.ds(pl.multiple_of(l * LANES, LANES), LANES)
@@ -166,26 +174,7 @@
         halo(2, out_grad.at[pl.ds(0, EDGE)], g_right, lax.rem(c + n_ctx - 1, n_ctx)),
     ]
 
-    def step(i, carry):
-        @pl.when(i + 2 < chunks)
-        def _():
-            for load in loads(i + 2):
-                load.start()
-
-        for load in loads(i):
-            load.wait()
-        interior(i)
-
-        @pl.when(jnp.logical_and(jnp.logical_not(first), i < early))
-        def _():
-            for send in sends(i):
-                send.start()
-
-        return carry
-
     filter_load.wait()
-    for load in loads(2):
-        load.start()
     for load in loads(0):
         load.wait()
     interior(0)
@@ -196,6 +185,10 @@
         for send in sends(0):
             send.start()
 
+    for i in range(3, len(groups)):
+        for load in loads(i):
+            load.start()
+
     @pl.when(c < n_ctx - 1)
     def _():
         for send in to_right:
@@ -215,7 +208,16 @@
         q_right[...] = jnp.zeros_like(q_right)
         g_right[...] = jnp.zeros_like(g_right)
 
-    lax.fori_loop(1, chunks, step, 0)
+    for i in range(1, len(groups)):
+        for load in loads(i):
+            load.wait()
+        interior(i)
+        if i < early:
+
+            @pl.when(jnp.logical_not(first))
+            def _():
+                for send in sends(i):
+                    send.start()
 
     @pl.when(c > 0)
     def _():
@@ -229,6 +231,11 @@
 
     dh[...] = jnp.zeros_like(dh)
     lax.fori_loop(0, width // LANES, edges, 0)
+
+    @pl.when(jnp.logical_not(first))
+    def _():
+        for send in edge_sends():
+            send.start()
 
     shares = []
     for d in range(1, n_ctx):
@@ -257,14 +264,9 @@
 
     @pl.when(jnp.logical_not(first))
     def _():
-        def late(i, carry):
+        for i in range(early, len(groups)):
             for send in sends(i):
                 send.start()
-            return carry
-
-        lax.fori_loop(early, chunks, late, 0)
-        for send in edge_sends():
-            send.start()
 
     @pl.when(last)
     def _():
@@ -291,23 +293,17 @@
 
     @pl.when(jnp.logical_not(first))
     def _():
-        def drained(i, carry):
+        for i in range(len(groups)):
             for send in sends(i):
                 send.wait_send()
-            return carry
-
-        lax.fori_loop(0, chunks, drained, 0)
         for send in edge_sends():
             send.wait_send()
 
     @pl.when(jnp.logical_not(last))
     def _():
-        def landed(i, carry):
+        for i in range(len(groups)):
             for send in sends(i):
                 send.wait_recv()
-            return carry
-
-        lax.fori_loop(0, chunks, landed, 0)
         for send in edge_sends():
             send.wait_recv()
 
@@ -316,7 +312,7 @@
     _, rows, width = query.shape
     taps = filters.shape[1]
     own = width // n_ctx
-    chunks = width // CHUNK
+    groups = len(groups_of(width))
     vmem = pl.BlockSpec(memory_space=pltpu.VMEM)
     operands = (trace_lengths, query[0], inner[0], out_grad[0], jnp.swapaxes(filters, 0, 1))
     f32, bf16, dma = jnp.float32, jnp.bfloat16, pltpu.SemaphoreType.DMA
@@ -344,12 +340,12 @@
             pltpu.VMEM((16, own // 2), bf16),
             pltpu.VMEM((16, own // 2), bf16),
             dma,
-            dma((3, chunks)),
+            dma((3, groups)),
             dma,
             dma((3,)),
             dma((3,)),
-            dma((2, chunks)),
-            dma((2, chunks)),
+            dma((2, groups)),
+            dma((2, groups)),
             dma((2,)),
             dma((2,)),
             dma((n_ctx - 1,)),

time: 57.9 us -> 57.3 us (0.990)
  Pallas kernels: 54.4 us -> 53.8 us
where the time goes in v4:
time: 57.3 us; the launch traced here: 57.1 us
  Pallas kernels  53.8 us (94%)
  local copies, waits for them, and re-layouts  2.66 us (5%)
  between operations  0.64 us (1%)
    pallas_call x1, Pallas kernels, local(): pl.pallas_call(functools.partial(kernel, n_pipe, n_ctx, trace_lengths.sha...  53.8 us
    unnamed x2, local copies, waits for them, and re-layouts  2.66 us

profile of v4, /device:TPU:1, one launch (start us, length us, event | category | flops | bytes accessed | tf_op | source)
XLA Modules:
  0.0 57.1 jit_solution(3693081918550690556)
XLA Ops:
  0.6 53.8 %grads_passed_on.1 = (bf16[2,1,128,8192]{3,2,1,0:T(8,128)(2,1)S(1)}, f32[7,1,4096]{2,1,0:T(1,128)S(1)}) custom-call(s32[1,2]{1,0:T(1,128)} %trace_lengths.1, bf16[128,8192]{1,0:T(8,128)(2,1)} %bitcast.6, bf16[128,8192]{1,0:T(8,128)(2,1)} %bitcast.7, bf16[128,8192]{1,0:T(8,128)(2,1)} %bitcast.8, f32[7,1,8192]{2,1,0:T(1,128)} %bitcast.9), custom_call_target="tpu_custom_call" | custom-call | tf_op jit(solution)/shard_map/grads_passed_on/pallas_call | solution.py:319
  54.5 2.0 %copy.9 = bf16[2,1,128,8192]{3,2,1,0:T(8,128)(2,1)} copy(bf16[2,1,128,8192]{3,2,1,0:T(8,128)(2,1)S(1)} %get-tuple-element.6) | data formatting | bytes 8388608
  56.5 0.6 %copy.10 = f32[1,7,4096]{2,0,1:T(1,128)} copy(f32[1,7,4096]{2,0,1:T(1,128)S(1)} %bitcast.5) | data formatting | bytes 229376

commit v5 on v4

--- a/solution.py
+++ b/solution.py
@@ -10,6 +10,7 @@
 MESH = pl.DeviceIdType.MESH
 EDGE = 16
 LANES = 128
+PARTS = 4
 FIRST_GROUPS = (256, 256, 512, 1024)
 GROUP = 2048
 
@@ -306,6 +307,20 @@
                 send.wait_recv()
         for send in edge_sends():
             send.wait_recv()
+
+
+def finish(arrived, summed, passed, grad, sem, grad_sem):
+    rows = arrived.shape[2]
+    part = rows // PARTS
+    copies = [pltpu.make_async_copy(summed, grad, grad_sem)]
+    for k in range(2):
+        for i in range(PARTS):
+            at = pl.ds(i * part, part)
+            copies.append(pltpu.make_async_copy(arrived.at[k, 0, at], passed.at[k, 0, at], sem.at[k, i]))
+    for copy in copies:
+        copy.start()
+    for copy in copies:
+        copy.wait()
 
 
 def local(n_pipe, n_ctx, query, inner, out_grad, filters, trace_lengths):
@@ -356,7 +371,16 @@
         compiler_params=pltpu.CompilerParams(collective_id=0, has_side_effects=True, vmem_limit_bytes=48 * 1024 * 1024),
         name="grads_passed_on",
     )(*(pltpu.with_memory_space_constraint(x, pltpu.HBM) for x in operands))
-    return arrived, jnp.swapaxes(summed, 0, 1)
+    passed, grad = pl.pallas_call(
+        finish,
+        out_shape=(jax.ShapeDtypeStruct((2, 1, rows, width), bf16), jax.ShapeDtypeStruct((taps, 1, own), f32)),
+        in_specs=[pl.BlockSpec(memory_space=pl.ANY)] * 2,
+        out_specs=(pl.BlockSpec(memory_space=pl.ANY),) * 2,
+        scratch_shapes=[dma((2, PARTS)), dma],
+        compiler_params=pltpu.CompilerParams(vmem_limit_bytes=1024 * 1024),
+        name="results_written",
+    )(*(pltpu.with_memory_space_constraint(x, pltpu.VMEM) for x in (arrived, summed)))
+    return passed, jnp.swapaxes(grad, 0, 1)
 
 
 def solution(mesh):

time: 57.3 us -> 56.8 us (level)
  local copies, waits for them, and re-layouts: 2.66 us -> 0 us
  Pallas kernels: 53.8 us -> 56 us
    unnamed x2 -> x0, local copies, waits for them, and re-layouts: 2.66 us -> none
    pallas_call x0 -> x1, Pallas kernels: none -> 2.12 us  [local(): pl.pallas_call(finish, out_shape=(jax.ShapeDtypeStruct((2, 1, rows, width...]
where the time goes in v5:
time: 56.8 us; the launch traced here: 56.6 us
  Pallas kernels  56 us (99%)
  between operations  0.64 us (1%)
    pallas_call x1, Pallas kernels, local(): pl.pallas_call(functools.partial(kernel, n_pipe, n_ctx, trace_lengths.sha...  53.8 us
    pallas_call x1, Pallas kernels, local(): pl.pallas_call(finish, out_shape=(jax.ShapeDtypeStruct((2, 1, rows, width...  2.12 us

profile of v5, /device:TPU:1, one launch (start us, length us, event | category | flops | bytes accessed | tf_op | source)
XLA Modules:
  0.0 56.6 jit_solution(1579395781504701130)
XLA Ops:
  0.6 53.8 %grads_passed_on.1 = (bf16[2,1,128,8192]{3,2,1,0:T(8,128)(2,1)S(1)}, f32[7,1,4096]{2,1,0:T(1,128)S(1)}) custom-call(s32[1,2]{1,0:T(1,128)} %trace_lengths.1, bf16[128,8192]{1,0:T(8,128)(2,1)} %bitcast.5, bf16[128,8192]{1,0:T(8,128)(2,1)} %bitcast.6, bf16[128,8192]{1,0:T(8,128)(2,1)} %bitcast.7, f32[7,1,8192]{2,1,0:T(1,128)} %bitcast.8), custom_call_target="tpu_custom_call" | custom-call | tf_op jit(solution)/shard_map/grads_passed_on/pallas_call | solution.py:334
  54.5 2.1 %results_written.1 = (bf16[2,1,128,8192]{3,2,1,0:T(8,128)(2,1)}, f32[7,1,4096]{2,1,0:T(1,128)}) custom-call(bf16[2,1,128,8192]{3,2,1,0:T(8,128)(2,1)S(1)} %get-tuple-element.6.arrived, f32[7,1,4096]{2,1,0:T(1,128)S(1)} %get-tuple-element.7.summed), custom_call_target="tpu_custom_call" | custom-call | tf_op jit(solution)/shard_map/results_written/pallas_call | solution.py:374

commit v6 on v5

--- a/solution.py
+++ b/solution.py
@@ -11,7 +11,7 @@
 EDGE = 16
 LANES = 128
 PARTS = 4
-FIRST_GROUPS = (256, 256, 512, 1024)
+FIRST_GROUPS = (128, 128, 256, 512, 1024)
 GROUP = 2048
 
 
@@ -57,19 +57,29 @@
             for k, (src, dst) in enumerate(((query, q_v), (inner, u_v), (out_grad, g_v)))
         ]
 
+    head = pl.ds(0, LANES)
+    rest = pl.ds(LANES, width - LANES)
+    filter_loads = [
+        pltpu.make_async_copy(filters.at[:, :, cols], f_v.at[:, :, cols], filter_sem.at[k])
+        for k, cols in enumerate((head, rest))
+    ]
     length_load = pltpu.make_async_copy(trace_lengths, lengths, length_sem)
     length_load.start()
-    filter_load = pltpu.make_async_copy(filters, f_v, filter_sem)
-    filter_load.start()
-    for i in range(3):
-        for load in loads(i):
-            load.start()
+    for load in loads(0):
+        load.start()
+    filter_loads[0].start()
 
     barrier = pltpu.get_barrier_semaphore()
     for other in (before, after, mirror):
         pl.semaphore_signal(barrier, inc=1, device_id={"pipe": other}, device_id_type=MESH)
     for d in range(1, n_ctx):
         pl.semaphore_signal(barrier, inc=1, device_id={"ctx": lax.rem(c + d, n_ctx)}, device_id_type=MESH)
+
+    filter_loads[1].start()
+    for i in range(1, 4):
+        for load in loads(i):
+            load.start()
+
 
     length_load.wait()
     ends = []
@@ -175,7 +185,7 @@
         halo(2, out_grad.at[pl.ds(0, EDGE)], g_right, lax.rem(c + n_ctx - 1, n_ctx)),
     ]
 
-    filter_load.wait()
+    filter_loads[0].wait()
     for load in loads(0):
         load.wait()
     interior(0)
@@ -186,7 +196,7 @@
         for send in sends(0):
             send.start()
 
-    for i in range(3, len(groups)):
+    for i in range(4, len(groups)):
         for load in loads(i):
             load.start()
 
@@ -209,6 +219,7 @@
         q_right[...] = jnp.zeros_like(q_right)
         g_right[...] = jnp.zeros_like(g_right)
 
+    filter_loads[1].wait()
     for i in range(1, len(groups)):
         for load in loads(i):
             load.wait()
@@ -356,7 +367,7 @@
             pltpu.VMEM((16, own // 2), bf16),
             dma,
             dma((3, groups)),
-            dma,
+            dma((2,)),
             dma((3,)),
             dma((3,)),
             dma((2, groups)),

time: 56.8 us -> 56.8 us (level)
  no operation moved by 1% of the time
where the time goes in v6:
time: 56.8 us; the launch traced here: 56.7 us
  Pallas kernels  56 us (99%)
  between operations  0.64 us (1%)
    pallas_call x1, Pallas kernels, local(): pl.pallas_call(functools.partial(kernel, n_pipe, n_ctx, trace_lengths.sha...  53.9 us
    pallas_call x1, Pallas kernels, local(): pl.pallas_call(finish, out_shape=(jax.ShapeDtypeStruct((2, 1, rows, width...  2.12 us

profile of v6, /device:TPU:1, one launch (start us, length us, event | category | flops | bytes accessed | tf_op | source)
XLA Modules:
  0.0 56.7 jit_solution(6247701522588620969)
XLA Ops:
  0.6 53.9 %grads_passed_on.1 = (bf16[2,1,128,8192]{3,2,1,0:T(8,128)(2,1)S(1)}, f32[7,1,4096]{2,1,0:T(1,128)S(1)}) custom-call(s32[1,2]{1,0:T(1,128)} %trace_lengths.1, bf16[128,8192]{1,0:T(8,128)(2,1)} %bitcast.5, bf16[128,8192]{1,0:T(8,128)(2,1)} %bitcast.6, bf16[128,8192]{1,0:T(8,128)(2,1)} %bitcast.7, f32[7,1,8192]{2,1,0:T(1,128)} %bitcast.8), custom_call_target="tpu_custom_call" | custom-call | tf_op jit(solution)/shard_map/grads_passed_on/pallas_call | solution.py:345
  54.6 2.1 %results_written.1 = (bf16[2,1,128,8192]{3,2,1,0:T(8,128)(2,1)}, f32[7,1,4096]{2,1,0:T(1,128)}) custom-call(bf16[2,1,128,8192]{3,2,1,0:T(8,128)(2,1)S(1)} %get-tuple-element.6.arrived, f32[7,1,4096]{2,1,0:T(1,128)S(1)} %get-tuple-element.7.summed), custom_call_target="tpu_custom_call" | custom-call | tf_op jit(solution)/shard_map/results_written/pallas_call | solution.py:385

commit v7 on v6

--- a/solution.py
+++ b/solution.py
@@ -328,8 +328,8 @@
         for i in range(PARTS):
             at = pl.ds(i * part, part)
             copies.append(pltpu.make_async_copy(arrived.at[k, 0, at], passed.at[k, 0, at], sem.at[k, i]))
-    for copy in copies:
-        copy.start()
+    for i, copy in enumerate(copies):
+        copy.start(priority=i % 2)
     for copy in copies:
         copy.wait()
 

time: 56.8 us -> 56.8 us (level)
  no operation moved by 1% of the time
where the time goes in v7:
time: 56.8 us; the launch traced here: 56.7 us
  Pallas kernels  56 us (99%)
  between operations  0.64 us (1%)
    pallas_call x1, Pallas kernels, local(): pl.pallas_call(functools.partial(kernel, n_pipe, n_ctx, trace_lengths.sha...  53.9 us
    pallas_call x1, Pallas kernels, local(): pl.pallas_call(finish, out_shape=(jax.ShapeDtypeStruct((2, 1, rows, width...  2.12 us

profile of v7, /device:TPU:1, one launch (start us, length us, event | category | flops | bytes accessed | tf_op | source)
XLA Modules:
  0.0 56.7 jit_solution(3837281132055011200)
XLA Ops:
  0.6 53.9 %grads_passed_on.1 = (bf16[2,1,128,8192]{3,2,1,0:T(8,128)(2,1)S(1)}, f32[7,1,4096]{2,1,0:T(1,128)S(1)}) custom-call(s32[1,2]{1,0:T(1,128)} %trace_lengths.1, bf16[128,8192]{1,0:T(8,128)(2,1)} %bitcast.5, bf16[128,8192]{1,0:T(8,128)(2,1)} %bitcast.6, bf16[128,8192]{1,0:T(8,128)(2,1)} %bitcast.7, f32[7,1,8192]{2,1,0:T(1,128)} %bitcast.8), custom_call_target="tpu_custom_call" | custom-call | tf_op jit(solution)/shard_map/grads_passed_on/pallas_call | solution.py:345
  54.6 2.1 %results_written.1 = (bf16[2,1,128,8192]{3,2,1,0:T(8,128)(2,1)}, f32[7,1,4096]{2,1,0:T(1,128)}) custom-call(bf16[2,1,128,8192]{3,2,1,0:T(8,128)(2,1)S(1)} %get-tuple-element.6.arrived, f32[7,1,4096]{2,1,0:T(1,128)S(1)} %get-tuple-element.7.summed), custom_call_target="tpu_custom_call" | custom-call | tf_op jit(solution)/shard_map/results_written/pallas_call | solution.py:385

commit v8 on v5

--- a/solution.py
+++ b/solution.py
@@ -40,7 +40,7 @@
     rows = query.shape[0]
     own = width // n_ctx
     groups = groups_of(width)
-    early = sum(start < width // 2 for start, _ in groups)
+    early = sum(start < width * 3 // 4 for start, _ in groups)
     s = lax.axis_index("pipe")
     c = lax.axis_index("ctx")
     first, last = s == 0, s == n_pipe - 1

time: 56.8 us -> 56.8 us (level)
  no operation moved by 1% of the time
where the time goes in v8:
time: 56.8 us; the launch traced here: 56.6 us
  Pallas kernels  56 us (99%)
  between operations  0.64 us (1%)
    pallas_call x1, Pallas kernels, local(): pl.pallas_call(functools.partial(kernel, n_pipe, n_ctx, trace_lengths.sha...  53.8 us
    pallas_call x1, Pallas kernels, local(): pl.pallas_call(finish, out_shape=(jax.ShapeDtypeStruct((2, 1, rows, width...  2.12 us

profile of v8, /device:TPU:1, one launch (start us, length us, event | category | flops | bytes accessed | tf_op | source)
XLA Modules:
  0.0 56.6 jit_solution(15483303025814246292)
XLA Ops:
  0.6 53.8 %grads_passed_on.1 = (bf16[2,1,128,8192]{3,2,1,0:T(8,128)(2,1)S(1)}, f32[7,1,4096]{2,1,0:T(1,128)S(1)}) custom-call(s32[1,2]{1,0:T(1,128)} %trace_lengths.1, bf16[128,8192]{1,0:T(8,128)(2,1)} %bitcast.5, bf16[128,8192]{1,0:T(8,128)(2,1)} %bitcast.6, bf16[128,8192]{1,0:T(8,128)(2,1)} %bitcast.7, f32[7,1,8192]{2,1,0:T(1,128)} %bitcast.8), custom_call_target="tpu_custom_call" | custom-call | tf_op jit(solution)/shard_map/grads_passed_on/pallas_call | solution.py:334
  54.5 2.1 %results_written.1 = (bf16[2,1,128,8192]{3,2,1,0:T(8,128)(2,1)}, f32[7,1,4096]{2,1,0:T(1,128)}) custom-call(bf16[2,1,128,8192]{3,2,1,0:T(8,128)(2,1)S(1)} %get-tuple-element.6.arrived, f32[7,1,4096]{2,1,0:T(1,128)S(1)} %get-tuple-element.7.summed), custom_call_target="tpu_custom_call" | custom-call | tf_op jit(solution)/shard_map/results_written/pallas_call | solution.py:374
